TPU v7x, 256 devices: a whole 4x4x8 slice. The times are simulated.
256 devices in a mesh: rep: 4 (over z_lo, core), fsdp: 64 (over x, z_hi, y).
Axes of the slice: x: 4, y: 4, z: 8 (z_hi: 4, z_lo: 2; z = z_hi * 2 + z_lo), core: 2. Of those that a mesh axis runs over, the one named last changes fastest.
Arguments:
- activations: bfloat16 [4, 3072, 4096], P('rep', 'fsdp'), may hold values from -6 to 6
- cotangent: bfloat16 [4, 14336, 3072], P('rep', 'fsdp'), may hold values from -6 to 6
- weight: bfloat16 [14336, 4096], P('fsdp', 'rep'), may hold values from -6 to 6
- first_moment: bfloat16 [4, 14336, 4096], P('rep', 'fsdp'), may hold values from -3 to 3
- second_moment: bfloat16 [4, 14336, 4096], P('rep', 'fsdp'), may hold values from 0.099609375 to 10
- momentum: float32 [14336, 4096], P('fsdp', 'rep'), may hold values from -2 to 2
- exponents: int32 [4, 14336, 32], P('rep', 'fsdp'), may hold values from -10 to -7
Outputs:
- new_weight: bfloat16 [14336, 4096], P('fsdp', 'rep')
- new_momentum: float32 [14336, 4096], P('fsdp', 'rep')
- new_first: bfloat16 [4, 14336, 4096], P('rep', 'fsdp')
- new_second: bfloat16 [4, 14336, 4096], P('rep', 'fsdp')
All inputs are finite; a program needn't handle non-finite values.
Results may differ from a plain program's by a relative error of at most 0.0039.
Values may be sent and summed in bfloat16 or wider, within the bound.
A program may use at most 128 MiB of HBM per device.

v0:
```python
import math

import jax
import jax.numpy as jnp
from jax import lax
from jax.sharding import PartitionSpec as P

beta_first = 0.9
beta_second = 0.95
inner_rate = 0.25
decay_rate = 0.1
epsilon = 1e-08
clip_limit = 448.0
outer_rate = 0.7
outer_beta = 0.9


def shards(activations, cotangent, weight, first_moment, second_moment, momentum, exponents):
    full_weight = lax.all_gather(weight, "rep", axis=1, tiled=True)
    row_count = full_weight.shape[0]
    full_width = full_weight.shape[1]
    cot_local = cotangent[0]
    factor = 1.0 / math.sqrt(full_width)
    tokens = lax.all_gather(activations, "fsdp", axis=1, tiled=True)[0]
    grad_sum = jnp.dot(cot_local, tokens, preferred_element_type=jnp.float32)
    gradient = grad_sum * factor
    new_first = (
        beta_first * first_moment[0].astype(jnp.float32) + (1.0 - beta_first) * gradient
    ).astype(jnp.bfloat16)
    new_second = (
        beta_second * second_moment[0].astype(jnp.float32)
        + (1.0 - beta_second) * gradient * gradient
    ).astype(jnp.bfloat16)
    step_size = inner_rate * (
        new_first.astype(jnp.float32) / (jnp.sqrt(new_second.astype(jnp.float32)) + epsilon)
        + decay_rate * full_weight.astype(jnp.float32)
    )
    blocks = exponents.shape[2]
    block_span = full_width // blocks
    exponent_f = exponents[0].astype(jnp.float32)
    shaped = step_size.reshape(row_count, blocks, block_span) * jnp.exp2(-exponent_f)[:, :, None]
    quantized = (
        jnp.clip(shaped, -clip_limit, clip_limit)
        .astype(jnp.bfloat16)
        .reshape(row_count, full_width)
    )
    scales = jnp.exp2(exponent_f).astype(jnp.bfloat16)
    quarter = weight.shape[1]
    count_rep = lax.axis_size("rep")
    every_quant, every_scale = (
        lax.all_gather(quantized[None], "rep", axis=0, tiled=True),
        lax.all_gather(scales[None], "rep", axis=0, tiled=True),
    )
    offset = lax.axis_index("rep") * quarter
    mine_quant = lax.dynamic_slice_in_dim(every_quant, offset, quarter, 2)
    mine_scale = lax.dynamic_slice_in_dim(
        every_scale, offset // block_span, quarter // block_span, 2
    )
    restored = (
        mine_quant.astype(jnp.float32).reshape(
            count_rep, row_count, quarter // block_span, block_span
        )
        * mine_scale.astype(jnp.float32)[..., None]
    )
    pseudo_grad = jnp.sum(restored, axis=0).reshape(row_count, quarter) / count_rep
    new_momentum = outer_beta * momentum + pseudo_grad
    new_weight = (
        weight.astype(jnp.float32) - outer_rate * (pseudo_grad + outer_beta * new_momentum)
    ).astype(jnp.bfloat16)
    return (new_weight, new_momentum, new_first[None], new_second[None])


def solution(mesh):
    in_specs = (
        P("rep", "fsdp", None),
        P("rep", "fsdp", None),
        P("fsdp", "rep"),
        P("rep", "fsdp", None),
        P("rep", "fsdp", None),
        P("fsdp", "rep"),
        P("rep", "fsdp", None),
    )
    out_specs = (P("fsdp", "rep"), P("fsdp", "rep"), P("rep", "fsdp", None), P("rep", "fsdp", None))
    return jax.shard_map(shards, mesh=mesh, in_specs=in_specs, out_specs=out_specs, check_vma=False)
```

profile of v0, /device:TPU:1, one launch (start us, length us, event | category | flops | bytes accessed | tf_op | source)
XLA Modules:
  0.0 378.0 jit_solution(12975229318009957510)
XLA Ops:
  7.2 0.0 copy-start
  7.2 0.0 all-gather.7.cloned.1.call-start
  7.2 0.7 all-gather.7.cloned.1.call-update
  7.9 0.0 all-gather.5.cloned.1.call-start
  8.0 0.7 all-gather.5.cloned.1.call-update
  8.7 0.0 all-gather.9.cloned.1.call-start
  8.7 0.8 exponential_bitcast_fusion
  9.5 0.1 copy.13
  9.6 34.1 %all-gather.7.cloned.1.call-done = bf16[224,4096]{1,0:T(8,128)(2,1)} async-done(((bf16[224,1024]{1,0:T(8,128)(2,1)}), bf16[224,4096]{1,0:T(8,128)(2,1)}) %all-gather.7.cloned.1.call-update) | async-done | bytes 1835024 | tf_op jit(solution)/shard_map/all_gather | solution.py:19
  43.7 230.0 %all-gather.5.cloned.1.call-done = bf16[1,3072,4096]{2,1,0:T(8,128)(2,1)} async-done(((bf16[1,48,4096]{2,1,0:T(8,128)(2,1)}), bf16[1,3072,4096]{2,1,0:T(8,128)(2,1)}) %all-gather.5.cloned.1.call-update) | async-done | bytes 25165840 | tf_op jit(solution)/shard_map/all_gather | solution.py:24
  273.7 1.0 mul.101
  274.7 0.0 copy-done
  274.7 0.0 copy-done.3
  274.7 0.5 copy-done.4
  275.2 16.4 %fusion.8 = (bf16[1,224,4096]{2,1,0:T(8,128)(2,1)}, bf16[224,4096]{1,0:T(8,128)(2,1)}, bf16[1,224,4096]{2,1,0:T(8,128)(2,1)}) fusion(bf16[1,224,4096]{2,1,0:T(8,128)(2,1)S(1)} %copy-done.3, f32[28,8,32,128]{3,2,1,0:T(8,128)S(1)} %bitcast.42, bf16[224,4096]{1,0:T(8,128)(2,1)} %all-gather.7.cloned.1.call-done, bf16[1,224,4096]{2,1,0:T(8,128)(2,1)S(1)} %copy-done.4, ...), kind=kOutput, calls=%fused_computation.17 | convolution fusion | flops 5658247168 | bytes 41222144 | tf_op jit(solution)/shard_map/dot_general | solution.py:25
  291.6 0.0 all-gather.9.cloned.1.call-update
  291.6 7.0 %all_gather.15 = bf16[4,224,32]{1,2,0:T(8,128)(2,1)S(1)} all-gather(bf16[1,224,32]{1,2,0:T(8,128)(2,1)S(1)} %get-tuple-element.10), channel_id=1, replica_groups=mesh['rep'=4,'fsdp'=64] {'rep'}, dimensions={0}, use_global_device_ids=true | all-gather | bytes 71680 | tf_op jit(solution)/shard_map/all_gather | solution.py:52
  298.7 0.2 copy.14
  298.8 2.5 mul.105
  301.3 5.0 %mul.106 = f32[4,224,1024]{2,1,0:T(8,128)} reshape(f32[4,224,8,128]{3,2,1,0:T(8,128)} %mul.105) | data formatting | bytes 7340032 | tf_op jit(solution)/shard_map/mul | solution.py:60
  306.3 60.5 %all-gather.9.cloned.1.call-done = bf16[896,4096]{1,0:T(8,128)(2,1)} async-done(((bf16[224,4096]{1,0:T(8,128)(2,1)}), bf16[896,4096]{1,0:T(8,128)(2,1)}) %all-gather.9.cloned.1.call-update) | async-done | bytes 7340048 | tf_op jit(solution)/shard_map/all_gather | solution.py:51
  366.8 3.3 multiply_reduce_fusion
  370.1 0.0 copy-done.1
  370.1 1.3 subtract_convert_fusion
  (6 shorter events, 0.0 us)
Async XLA Ops:
  7.2 267.5 %copy-start = (bf16[1,224,3072]{2,1,0:T(8,128)(2,1)S(1)}, bf16[1,224,3072]{2,1,0:T(8,128)(2,1)}, u32[]{:S(2)}) copy-start(bf16[1,224,3072]{2,1,0:T(8,128)(2,1)} %param.8) | copy-start | bytes 4128772
  7.2 267.5 %copy-start.3 = (bf16[1,224,4096]{2,1,0:T(8,128)(2,1)S(1)}, bf16[1,224,4096]{2,1,0:T(8,128)(2,1)}, u32[]{:S(2)}) copy-start(bf16[1,224,4096]{2,1,0:T(8,128)(2,1)} %param.11) | copy-start | bytes 5505028
  7.2 36.5 %all-gather.7.cloned.1.call-start = ((), (), s32[]{:S(2)}) async-start(), calls=%async_computation.1 | async-start | bytes 2293760 | tf_op jit(solution)/shard_map/all_gather | solution.py:19
  7.9 265.7 %all-gather.5.cloned.1.call-start = ((), (), s32[]{:S(2)}) async-start(), calls=%async_computation | async-start | bytes 25559040 | tf_op jit(solution)/shard_map/all_gather | solution.py:24
  8.7 358.1 %all-gather.9.cloned.1.call-start = ((), (), s32[]{:S(2)}) async-start(), calls=%async_computation.2 | async-start | bytes 9175040 | tf_op jit(solution)/shard_map/all_gather | solution.py:51
  273.7 1.5 copy-start.4
  306.2 63.8 %copy-start.1 = (bf16[224,1024]{1,0:T(8,128)(2,1)S(1)}, bf16[224,1024]{1,0:T(8,128)(2,1)}, u32[]{:S(2)}) copy-start(bf16[224,1024]{1,0:T(8,128)(2,1)} %param.9) | copy-start | bytes 1376260
  306.2 63.8 %copy-start.2 = (f32[224,1024]{1,0:T(8,128)S(1)}, f32[224,1024]{1,0:T(8,128)}, u32[]{:S(2)}) copy-start(f32[224,1024]{1,0:T(8,128)} %param.12) | copy-start | bytes 2752516
Sparse Core Ops, SparseCore 0:
  9.8 33.7 all-gather.6
  46.9 226.6 all-gather.4
  291.7 74.9 all-gather.8
where the time goes:
time: 378 us
  waiting for transfers between devices  326 us (86%)
  matrix products  16.4 us (4%)
  between operations  13.8 us (4%)
  local copies, waits for them, and re-layouts  9.18 us (2%)
  blocking collectives  6.99 us (2%)
  other arithmetic  5.46 us (1%)
    all_gather x1, waiting for transfers between devices, shards(): tokens = lax.all_gather(activations, 'fsdp', axis=1, tiled=True)[0]  230 us
    all_gather x1, waiting for transfers between devices, shards(): lax.all_gather(quantized[None], 'rep', axis=0, tiled=True)  60.5 us
    all_gather x1, waiting for transfers between devices, shards(): full_weight = lax.all_gather(weight, 'rep', axis=1, tiled=True)  34.1 us
    dot_general x1, matrix products, shards(): grad_sum = jnp.dot(cot_local, tokens, preferred_element_type=jnp.float32)  16.4 us
  transfers between devices with their start and end apart: 3, of which 3 were waited for; matrix products, arithmetic and copies ran while one was open for 2% of the time, Pallas kernels for 0%

commit v1 on v0

v1 whole, which is shorter than its diff:
```python
import functools
import math

import jax
import jax.numpy as jnp
from jax import lax
from jax.experimental import pallas as pl
from jax.experimental.pallas import tpu as pltpu
from jax.sharding import PartitionSpec as P

beta_first = 0.9
beta_second = 0.95
inner_rate = 0.25
decay_rate = 0.1
epsilon = 1e-08
clip_limit = 448.0
outer_rate = 0.7
outer_beta = 0.9

MESH = pl.DeviceIdType.MESH
CHUNKS = 4
TILE = 32


def kernel(
    act, cot, wgt, first, second, mom, expo,
    out_weight, out_mom, out_first, out_second,
    cbuf, abuf, fbuf, sbuf, wbuf, mbuf, nfbuf, nsbuf, nwbuf, nmbuf,
    gsend, grecv, usend, urecv, ebuf, limbuf,
    load_sem, own_sem, out_sem,
    cs_sem, cr_sem, as_sem, ar_sem, zs_sem, zr_sem, bs_sem, br_sem,
    gs_sem, gr_sem, us_sem, ur_sem, es_sem, er_sem,
):
    rows, width = first.shape
    count = act.shape[0]
    quarter = width // 4
    cols = quarter // CHUNKS
    half = rows // 2
    factor = 1.0 / math.sqrt(width)

    rep = lax.axis_index("rep")
    place = lax.axis_index("fsdp")
    c = rep % 2
    x, z, y = place // 16, (place // 4) % 4, place % 4
    a = y * (1 - c) + x * c
    b = x * (1 - c) + y * c

    def device(a_, b_, z_):
        return (rep, (b_ * (1 - c) + a_ * c) * 16 + z_ * 4 + a_ * (1 - c) + b_ * c)

    def off(i, d):
        return (i + d + 4) % 4

    a_dev = {d: device(off(a, d), b, z) for d in (1, 2, 3)}
    b_dev = {d: device(a, off(b, d), z) for d in (1, 3)}
    z_dev = {d: device(a, b, off(z, d)) for d in (1, 3)}
    r_dev = {d: (off(rep, d), place) for d in (1, 2, 3)}

    barrier = pltpu.get_barrier_semaphore()
    partners = [*a_dev.values(), *b_dev.values(), *z_dev.values(), *r_dev.values()]
    for dev in partners:
        pl.semaphore_signal(barrier, inc=1, device_id=dev, device_id_type=MESH)

    loads = [
        pltpu.make_async_copy(src, dst, load_sem.at[i])
        for i, (src, dst) in enumerate(
            ((cot, cbuf.at[0]), (first, fbuf), (second, sbuf), (wgt, wbuf), (mom, mbuf), (expo_own(expo, rep), ebuf.at[rep]))
        )
    ]

    def unit(j, a_, b_, z_):
        return abuf.at[j, b_ * (1 - c) + a_ * c, z_, a_ * (1 - c) + b_ * c]

    own = [
        pltpu.make_async_copy(
            act.at[:, pl.ds(pl.multiple_of(a * quarter + j * cols, cols), cols)], unit(j, a, b, z), own_sem.at[j]
        )
        for j in range(CHUNKS)
    ]
    for copy in own + loads:
        copy.start()

    pl.semaphore_wait(barrier, len(partners))

    pending = []

    def remote(src, dst, send, recv, dev):
        copy = pltpu.make_async_remote_copy(
            src_ref=src, dst_ref=dst, send_sem=send, recv_sem=recv, device_id=dev, device_id_type=MESH
        )
        return copy

    def send(*args):
        copy = remote(*args)
        copy.start()
        pending.append(copy)

    def arrived(dst, recv):
        remote(dst, dst, recv, recv, a_dev[1]).wait_recv()

    for j in range(CHUNKS):
        for d in (2, 1, 3):
            send(
                act.at[:, pl.ds(pl.multiple_of(off(a, d) * quarter + j * cols, cols), cols)],
                unit(j, a, b, z), as_sem.at[j, d - 1], ar_sem.at[j, d - 1], a_dev[d],
            )
    halves = (pl.ds(0, half), pl.ds(half, half))
    for i, (to, slot, h) in enumerate(((1, 1, 0), (3, 3, 1), (1, 1, 1), (3, 3, 0))):
        send(cot.at[halves[h]], cbuf.at[slot, halves[h]], cs_sem.at[i], cr_sem.at[i], a_dev[to])
    for d in (1, 2, 3):
        send(expo_own(expo, off(rep, d)), ebuf.at[rep], es_sem.at[d - 1], er_sem.at[d - 1], r_dev[d])

    def block(j, b_, z_, role):
        return abuf.at[j, b_, z_] if role == 0 else abuf.at[j, :, z_, b_]

    def send_block(j, b_, z_, ssem, rsem, dev):
        for role in (0, 1):
            @pl.when(c == role)
            def _(role=role):
                ref = block(j, b_, z_, role)
                remote(ref, ref, ssem, rsem, dev).start()
        pending.append(remote(block(j, b_, z_, 0), block(j, b_, z_, 0), ssem, rsem, dev))

    def block_arrived(j, b_, z_, rsem):
        for role in (0, 1):
            @pl.when(c == role)
            def _(role=role):
                arrived(block(j, b_, z_, role), rsem)

    for j in range(CHUNKS):
        own[j].wait()
        for d in (1, 2, 3):
            arrived(unit(j, off(a, -d), b, z), ar_sem.at[j, d - 1])
        send_block(j, b, z, zs_sem.at[j, 0], zr_sem.at[j, 0], z_dev[1])
        send_block(j, b, z, zs_sem.at[j, 1], zr_sem.at[j, 1], z_dev[3])

    def z_two(j):
        block_arrived(j, b, off(z, -1), zr_sem.at[j, 0])
        block_arrived(j, b, off(z, 1), zr_sem.at[j, 1])
        if j % 2 == 0:
            send_block(j, b, off(z, -1), zs_sem.at[j, 2], zr_sem.at[j, 2], z_dev[1])
        else:
            send_block(j, b, off(z, 1), zs_sem.at[j, 2], zr_sem.at[j, 2], z_dev[3])

    def z_three(j):
        block_arrived(j, b, off(z, 2), zr_sem.at[j, 2])

    z_two(0)
    z_two(1)
    arrived(cbuf.at[1, halves[0]], cr_sem.at[0])
    send(cbuf.at[1, halves[0]], cbuf.at[2, halves[0]], cs_sem.at[4], cr_sem.at[4], a_dev[1])
    arrived(cbuf.at[3, halves[1]], cr_sem.at[1])
    send(cbuf.at[3, halves[1]], cbuf.at[2, halves[1]], cs_sem.at[5], cr_sem.at[5], a_dev[3])
    z_two(2)
    z_two(3)
    arrived(cbuf.at[1, halves[1]], cr_sem.at[2])
    arrived(cbuf.at[3, halves[0]], cr_sem.at[3])

    plane = [z, off(z, -1), off(z, 1), off(z, 2)]

    def b_one(j):
        z_three(j)
        for k in range(4):
            send_block(j, b, plane[k], bs_sem.at[j, 0, k], br_sem.at[j, 0, k], b_dev[1])
            send_block(j, b, plane[k], bs_sem.at[j, 1, k], br_sem.at[j, 1, k], b_dev[3])

    def b_two(j):
        for k in range(4):
            block_arrived(j, off(b, -1), plane[k], br_sem.at[j, 0, k])
            if k in (0, 3):
                send_block(j, off(b, -1), plane[k], bs_sem.at[j, 2, k], br_sem.at[j, 2, k], b_dev[1])
            block_arrived(j, off(b, 1), plane[k], br_sem.at[j, 1, k])
            if k in (1, 2):
                send_block(j, off(b, 1), plane[k], bs_sem.at[j, 2, k], br_sem.at[j, 2, k], b_dev[3])

    def b_three(j):
        for k in range(4):
            block_arrived(j, off(b, 2), plane[k], br_sem.at[j, 2, k])

    tokens = 64 * count

    def product(j):
        def one(i, carry):
            s = (i + 2) % 4
            got = jnp.dot(cbuf[s], abuf[j].reshape(tokens, cols), preferred_element_type=jnp.float32)
            gsend[j, s] = (got * factor).astype(jnp.bfloat16)

            @pl.when(s > 0)
            def _():
                remote(
                    gsend.at[j, s], grecv.at[j, a], gs_sem.at[j, s], gr_sem.at[j, s],
                    device(off(a, -s), b, z),
                ).start()

            return carry

        lax.fori_loop(0, 4, one, 0)
        for s in (1, 2, 3):
            pending.append(remote(gsend.at[j, s], grecv.at[j, a], gs_sem.at[j, s], gr_sem.at[j, s], a_dev[1]))
        grecv[j, a] = gsend[j, 0]

    def inner(j):
        for s in (1, 2, 3):
            arrived(grecv.at[j, off(a, s)], gr_sem.at[j, s])

        def one(i, carry):
            span = pl.ds(pl.multiple_of(i * TILE, TILE), TILE)
            for q in range(4):
                where = pl.ds(q * quarter + j * cols, cols)
                gradient = grecv[j, q, span].astype(jnp.float32)
                new_first = (
                    beta_first * fbuf[span, where].astype(jnp.float32) + (1.0 - beta_first) * gradient
                ).astype(jnp.bfloat16)
                new_second = (
                    beta_second * sbuf[span, where].astype(jnp.float32)
                    + (1.0 - beta_second) * gradient * gradient
                ).astype(jnp.bfloat16)
                nfbuf[span, where] = new_first
                nsbuf[span, where] = new_second
                ratio = new_first.astype(jnp.float32) / (jnp.sqrt(new_second.astype(jnp.float32)) + epsilon)
                usend[j, q, span] = ratio.astype(jnp.bfloat16)
            urecv[j, rep, span] = usend[j, rep, span]
            return carry

        lax.fori_loop(0, rows // TILE, one, 0)
        for d in (2, 3, 1):
            send(usend.at[j, off(rep, d)], urecv.at[j, rep], us_sem.at[j, d - 1], ur_sem.at[j, d - 1], r_dev[d])

    def outer(j):
        blocks = ebuf.shape[1]
        span_of = lax.broadcasted_iota(jnp.int32, (blocks, cols), 1) // (quarter // blocks) + j * (cols * blocks // quarter)
        spread = (span_of == lax.broadcasted_iota(jnp.int32, (blocks, cols), 0)).astype(jnp.float32).astype(jnp.bfloat16)
        for r in range(4):
            limits = (clip_limit * jnp.exp2(ebuf[r].astype(jnp.float32))).astype(jnp.bfloat16)
            limbuf[r] = lax.dot_general(
                limits, spread, (((0,), (0,)), ((), ())), preferred_element_type=jnp.float32
            )
        for d in (1, 2, 3):
            arrived(urecv.at[j, off(rep, -d)], ur_sem.at[j, d - 1])

        def one(i, carry):
            span = pl.ds(pl.multiple_of(i * TILE, TILE), TILE)
            where = pl.ds(j * cols, cols)
            weight = wbuf[span, where].astype(jnp.float32)
            total = jnp.zeros_like(weight)
            for r in range(4):
                delta = inner_rate * (urecv[j, r, span].astype(jnp.float32) + decay_rate * weight)
                limit = limbuf[r, span]
                total = total + jnp.minimum(jnp.maximum(delta, -limit), limit)
            pseudo = total * 0.25
            new_mom = outer_beta * mbuf[span, where] + pseudo
            nmbuf[span, where] = new_mom
            nwbuf[span, where] = (weight - outer_rate * (pseudo + outer_beta * new_mom)).astype(jnp.bfloat16)
            return carry

        lax.fori_loop(0, rows // TILE, one, 0)

    def ready(j):
        if j == 0:
            arrived(cbuf.at[2, halves[0]], cr_sem.at[4])
            arrived(cbuf.at[2, halves[1]], cr_sem.at[5])
            loads[0].wait()
        product(j)

    b_one(0)
    b_one(1)
    b_two(0)
    b_one(2)
    b_two(1)
    b_three(0)
    ready(0)
    b_one(3)
    b_two(2)
    b_three(1)
    ready(1)
    for copy in loads[1:]:
        copy.wait()
    for d in (1, 2, 3):
        arrived(ebuf.at[off(rep, -d)], er_sem.at[d - 1])
    inner(0)
    b_two(3)
    b_three(2)
    ready(2)
    inner(1)
    outer(0)
    b_three(3)
    ready(3)
    inner(2)
    outer(1)
    inner(3)
    outs = [
        pltpu.make_async_copy(nfbuf, out_first, out_sem.at[0]),
        pltpu.make_async_copy(nsbuf, out_second, out_sem.at[1]),
    ]
    for copy in outs:
        copy.start()
    outer(2)
    outer(3)
    last = [
        pltpu.make_async_copy(nwbuf, out_weight, out_sem.at[2]),
        pltpu.make_async_copy(nmbuf, out_mom, out_sem.at[3]),
    ]
    for copy in last:
        copy.start()
    for copy in pending:
        copy.wait_send()
    for copy in outs + last:
        copy.wait()


def expo_own(expo, q):
    blocks = expo.shape[0] // 4
    return expo.at[pl.ds(pl.multiple_of(q * blocks, blocks), blocks)]


def shards(activations, cotangent, weight, first_moment, second_moment, momentum, exponents):
    act, cot, first, second = activations[0], cotangent[0], first_moment[0], second_moment[0]
    expo = exponents[0].T
    rows, width = first.shape
    count, tokens = act.shape[0], cot.shape[1]
    quarter = weight.shape[1]
    cols = quarter // CHUNKS
    bf16, f32 = jnp.bfloat16, jnp.float32
    dma = pltpu.SemaphoreType.DMA
    new_weight, new_mom, new_first, new_second = pl.pallas_call(
        kernel,
        out_shape=(
            jax.ShapeDtypeStruct(weight.shape, bf16),
            jax.ShapeDtypeStruct(momentum.shape, f32),
            jax.ShapeDtypeStruct(first.shape, bf16),
            jax.ShapeDtypeStruct(second.shape, bf16),
        ),
        in_specs=[pl.BlockSpec(memory_space=pl.ANY)] * 7,
        out_specs=(pl.BlockSpec(memory_space=pl.ANY),) * 4,
        scratch_shapes=[
            pltpu.VMEM((4, rows, tokens), bf16),
            pltpu.VMEM((CHUNKS, 4, 4, 4, count, cols), bf16),
            pltpu.VMEM((rows, width), bf16),
            pltpu.VMEM((rows, width), bf16),
            pltpu.VMEM((rows, quarter), bf16),
            pltpu.VMEM((rows, quarter), f32),
            pltpu.VMEM((rows, width), bf16),
            pltpu.VMEM((rows, width), bf16),
            pltpu.VMEM((rows, quarter), bf16),
            pltpu.VMEM((rows, quarter), f32),
            pltpu.VMEM((CHUNKS, 4, rows, cols), bf16),
            pltpu.VMEM((CHUNKS, 4, rows, cols), bf16),
            pltpu.VMEM((CHUNKS, 4, rows, cols), bf16),
            pltpu.VMEM((CHUNKS, 4, rows, cols), bf16),
            pltpu.VMEM((4, expo.shape[0] // 4, rows), jnp.int32),
            pltpu.VMEM((4, rows, cols), f32),
            dma((6,)), dma((CHUNKS,)), dma((4,)),
            dma((6,)), dma((6,)),
            dma((CHUNKS, 3)), dma((CHUNKS, 3)),
            dma((CHUNKS, 3)), dma((CHUNKS, 3)),
            dma((CHUNKS, 3, 4)), dma((CHUNKS, 3, 4)),
            dma((CHUNKS, 4)), dma((CHUNKS, 4)),
            dma((CHUNKS, 3)), dma((CHUNKS, 3)),
            dma((3,)), dma((3,)),
        ],
        compiler_params=pltpu.CompilerParams(
            collective_id=0, has_side_effects=True, vmem_limit_bytes=52 * 1024 * 1024
        ),
        cost_estimate=pl.CostEstimate(flops=2 * rows * tokens * width, bytes_accessed=14_000_000, transcendentals=rows * width),
    )(act, cot, weight, first, second, momentum, expo)
    return (new_weight, new_mom, new_first[None], new_second[None])


def solution(mesh):
    in_specs = (
        P("rep", "fsdp", None),
        P("rep", "fsdp", None),
        P("fsdp", "rep"),
        P("rep", "fsdp", None),
        P("rep", "fsdp", None),
        P("fsdp", "rep"),
        P("rep", "fsdp", None),
    )
    out_specs = (P("fsdp", "rep"), P("fsdp", "rep"), P("rep", "fsdp", None), P("rep", "fsdp", None))
    return jax.shard_map(shards, mesh=mesh, in_specs=in_specs, out_specs=out_specs, check_vma=False)
```

time: 378 us -> 102 us (0.27)
  waiting for transfers between devices: 326 us -> 0 us
  Pallas kernels: 0 us -> 92.3 us
  matrix products: 16.4 us -> 0 us
  between operations: 13.8 us -> 0.66 us
  blocking collectives: 6.99 us -> 0 us
  other arithmetic: 5.46 us -> 0 us
    all_gather x3 -> x0, waiting for transfers between devices: 325 us -> none  [the longest x1 230 us: shards(): tokens = lax.all_gather(activations, 'fsdp', axis=1, tiled=True)[0]]
    pallas_call x0 -> x1, Pallas kernels: none -> 92.3 us  [shards(): pl.pallas_call(kernel, out_shape=(jax.ShapeDtypeStruct(weight.shape, bf16...]
    dot_general x1 -> x0, matrix products: 16.4 us -> none  [shards(): grad_sum = jnp.dot(cot_local, tokens, preferred_element_type=jnp.float32)]
    unnamed x10 -> x14, local copies, waits for them, and re-layouts: 0.5 us -> 9.13 us
    mul x3 -> x0, local copies, waits for them, and re-layouts: 8.41 us -> none  [the longest x2 7.41 us: shards(): mine_quant.astype(jnp.float32)]
    all_gather x1 -> x0, blocking collectives: 6.99 us -> none  [shards(): lax.all_gather(scales[None], 'rep', axis=0, tiled=True)]
  transfers between devices with their start and end apart: 3 -> 0, of which waited for: 3 -> 0; matrix products, arithmetic and copies ran while one was open for 2% -> 0% of each run, Pallas kernels for 0% -> 0%
where the time goes in v1:
time: 102 us
  Pallas kernels  92.3 us (90%)
  local copies, waits for them, and re-layouts  9.13 us (9%)
    pallas_call x1, Pallas kernels, shards(): pl.pallas_call(kernel, out_shape=(jax.ShapeDtypeStruct(weight.shape, bf16...  92.3 us
    unnamed x14, local copies, waits for them, and re-layouts  9.13 us

profile of v1, /device:TPU:1, one launch (start us, length us, event | category | flops | bytes accessed | tf_op | source)
XLA Modules:
  0.0 102.1 jit_solution(15802337466281800421)
XLA Ops:
  0.6 0.0 copy-start
  0.6 1.0 copy-done
  1.7 0.0 copy-start.1
  1.7 1.0 copy-done.1
  2.6 0.0 copy-start.2
  2.7 0.8 copy-done.2
  3.4 92.3 %shard_map.102 = (bf16[224,1024]{1,0:T(8,128)(2,1)S(1)}, f32[224,1024]{1,0:T(8,128)}, bf16[224,4096]{1,0:T(8,128)(2,1)}, bf16[224,4096]{1,0:T(8,128)(2,1)}) custom-call(bf16[48,4096]{1,0:T(8,128)(2,1)S(1)} %bitcast.9, bf16[224,3072]{1,0:T(8,128)(2,1)} %bitcast.15, bf16[224,1024]{1,0:T(8,128)(2,1)S(1)} %copy-done, bf16[224,4096]{1,0:T(8,128)(2,1)} %bitcast.13, ...), custom_call_target="tpu_custom_call" | custom-call | flops 5637144576 | bytes 14000000 | tf_op jit(solution)/shard_map/pallas_call | solution.py:325
  95.8 0.0 copy-start.4
  95.8 0.8 copy.15
  96.5 2.2 %copy.16 = f32[224,1024]{1,0:T(8,128)} copy(f32[224,1024]{1,0:T(8,128)} %get-tuple-element.17) | data formatting | bytes 1835008
  98.7 0.0 copy-done.4
  98.7 0.0 copy-start.3
  98.7 1.2 %copy.17 = bf16[1,224,4096]{2,1,0:T(8,128)(2,1)} copy(bf16[1,224,4096]{2,1,0:T(8,128)(2,1)S(1)} %bitcast.12) | data formatting | bytes 3670016
  100.0 0.9 copy-done.3
  100.9 1.2 %copy.18 = bf16[1,224,4096]{2,1,0:T(8,128)(2,1)} copy(bf16[1,224,4096]{2,1,0:T(8,128)(2,1)S(1)} %bitcast.11) | data formatting | bytes 3670016
Async XLA Ops:
  0.6 1.0 copy-start
  1.7 1.0 copy-start.1
  2.6 0.8 copy-start.2
  95.8 3.0 %copy-start.4 = (bf16[224,4096]{1,0:T(8,128)(2,1)S(1)}, bf16[224,4096]{1,0:T(8,128)(2,1)}, u32[]{:S(2)}) copy-start(bf16[224,4096]{1,0:T(8,128)(2,1)} %get-tuple-element.10) | copy-start | bytes 5505028
  98.7 2.2 %copy-start.3 = (bf16[224,4096]{1,0:T(8,128)(2,1)S(1)}, bf16[224,4096]{1,0:T(8,128)(2,1)}, u32[]{:S(2)}) copy-start(bf16[224,4096]{1,0:T(8,128)(2,1)} %get-tuple-element.11) | copy-start | bytes 5505028

commit v2 on v1

v2 whole, which is shorter than its diff:
```python
import functools
import math

import jax
import jax.numpy as jnp
from jax import lax
from jax.experimental import pallas as pl
from jax.experimental.pallas import tpu as pltpu
from jax.sharding import PartitionSpec as P

beta_first = 0.9
beta_second = 0.95
inner_rate = 0.25
decay_rate = 0.1
epsilon = 1e-08
clip_limit = 448.0
outer_rate = 0.7
outer_beta = 0.9

MESH = pl.DeviceIdType.MESH
PARTS = (256, 256, 256, 256)
CHUNKS = len(PARTS)
STARTS = tuple(sum(PARTS[:j]) for j in range(CHUNKS))
TILE = 32
SIDES = (0, 1, 1, 0)


def kernel(
    act, cot, wgt, first, second, mom, expo,
    out_weight, out_mom, out_first, out_second,
    cbuf, abuf, fbuf, sbuf, wbuf, mbuf,
    gsend, grecv, usend, urecv, ebuf, limbuf,
    load_sem, own_sem,
    cs_sem, cr_sem, as_sem, ar_sem, zs_sem, zr_sem, bs_sem, br_sem,
    gs_sem, gr_sem, us_sem, ur_sem, es_sem, er_sem,
):
    rows, width = first.shape
    count = act.shape[0]
    quarter = width // 4
    half = rows // 2
    factor = 1.0 / math.sqrt(width)

    rep = lax.axis_index("rep")
    place = lax.axis_index("fsdp")
    c = rep % 2
    x, z, y = place // 16, (place // 4) % 4, place % 4
    a = y * (1 - c) + x * c
    b = x * (1 - c) + y * c

    def device(a_, b_, z_):
        return (rep, (b_ * (1 - c) + a_ * c) * 16 + z_ * 4 + a_ * (1 - c) + b_ * c)

    def off(i, d):
        return (i + d + 4) % 4

    a_dev = {d: device(off(a, d), b, z) for d in (1, 2, 3)}
    b_dev = {d: device(a, off(b, d), z) for d in (1, 3)}
    z_dev = {d: device(a, b, off(z, d)) for d in (1, 3)}
    r_dev = {d: (off(rep, d), place) for d in (1, 2, 3)}

    barrier = pltpu.get_barrier_semaphore()
    partners = [*a_dev.values(), *b_dev.values(), *z_dev.values(), *r_dev.values()]
    for dev in partners:
        pl.semaphore_signal(barrier, inc=1, device_id=dev, device_id_type=MESH)

    loads = [
        pltpu.make_async_copy(src, dst, load_sem.at[i])
        for i, (src, dst) in enumerate(
            ((cot, cbuf.at[0]), (first, fbuf), (second, sbuf), (wgt, wbuf), (mom, mbuf), (expo_own(expo, rep), ebuf.at[rep]))
        )
    ]

    def unit(j, a_, b_, z_):
        return abuf[j].at[b_ * (1 - c) + a_ * c, z_, a_ * (1 - c) + b_ * c]

    own = [
        pltpu.make_async_copy(
            act.at[:, pl.ds(pl.multiple_of(a * quarter + STARTS[j], 128), PARTS[j])], unit(j, a, b, z), own_sem.at[j]
        )
        for j in range(CHUNKS)
    ]
    for copy in own + loads:
        copy.start()

    pl.semaphore_wait(barrier, len(partners))

    pending = []

    def remote(src, dst, send, recv, dev):
        copy = pltpu.make_async_remote_copy(
            src_ref=src, dst_ref=dst, send_sem=send, recv_sem=recv, device_id=dev, device_id_type=MESH
        )
        return copy

    def send(*args):
        copy = remote(*args)
        copy.start()
        pending.append(copy)

    def arrived(dst, recv):
        remote(dst, dst, recv, recv, a_dev[1]).wait_recv()

    def act_out(j):
        for d in (2, 1, 3):
            send(
                act.at[:, pl.ds(pl.multiple_of(off(a, d) * quarter + STARTS[j], 128), PARTS[j])],
                unit(j, a, b, z), as_sem.at[j, d - 1], ar_sem.at[j, d - 1], a_dev[d],
            )

    halves = (pl.ds(0, half), pl.ds(half, half))

    def cot_out(i):
        for k, (to, slot, h) in enumerate((((1, 1, 0), (3, 3, 1)), ((1, 1, 1), (3, 3, 0)))[i]):
            send(cot.at[halves[h]], cbuf.at[slot, halves[h]], cs_sem.at[2 * i + k], cr_sem.at[2 * i + k], a_dev[to])

    for d in (1, 2, 3):
        send(expo_own(expo, off(rep, d)), ebuf.at[rep], es_sem.at[d - 1], er_sem.at[d - 1], r_dev[d])

    def block(j, b_, z_, role):
        return abuf[j].at[b_, z_] if role == 0 else abuf[j].at[:, z_, b_]

    def send_block(j, b_, z_, ssem, rsem, dev):
        for role in (0, 1):
            @pl.when(c == role)
            def _(role=role):
                ref = block(j, b_, z_, role)
                remote(ref, ref, ssem, rsem, dev).start()
        pending.append(remote(block(j, b_, z_, 0), block(j, b_, z_, 0), ssem, rsem, dev))

    def block_arrived(j, b_, z_, rsem):
        for role in (0, 1):
            @pl.when(c == role)
            def _(role=role):
                arrived(block(j, b_, z_, role), rsem)

    def z_one(j):
        own[j].wait()
        for d in (1, 2, 3):
            arrived(unit(j, off(a, -d), b, z), ar_sem.at[j, d - 1])
        send_block(j, b, z, zs_sem.at[j, 0], zr_sem.at[j, 0], z_dev[1])
        send_block(j, b, z, zs_sem.at[j, 1], zr_sem.at[j, 1], z_dev[3])

    def z_two(j):
        d = (-1, 1)[j % 2]
        block_arrived(j, b, off(z, d), zr_sem.at[j, j % 2])
        send_block(j, b, off(z, d), zs_sem.at[j, 2], zr_sem.at[j, 2], z_dev[-d % 4])
        block_arrived(j, b, off(z, -d), zr_sem.at[j, 1 - j % 2])

    def z_three(j):
        block_arrived(j, b, off(z, 2), zr_sem.at[j, 2])

    def cot_one(d):
        slot = (1, 3)[d]
        arrived(cbuf.at[slot, halves[d]], cr_sem.at[d])
        send(cbuf.at[slot, halves[d]], cbuf.at[2, halves[d]], cs_sem.at[4 + d], cr_sem.at[4 + d], a_dev[slot])

    def cot_two():
        arrived(cbuf.at[1, halves[1]], cr_sem.at[2])
        arrived(cbuf.at[3, halves[0]], cr_sem.at[3])

    def cot_three():
        arrived(cbuf.at[2, halves[0]], cr_sem.at[4])
        arrived(cbuf.at[2, halves[1]], cr_sem.at[5])

    plane = [z, off(z, -1), off(z, 1), off(z, 2)]

    def b_one(j, k):
        send_block(j, b, plane[k], bs_sem.at[j, 0, k], br_sem.at[j, 0, k], b_dev[1])
        send_block(j, b, plane[k], bs_sem.at[j, 1, k], br_sem.at[j, 1, k], b_dev[3])

    def b_two(j, k):
        d = SIDES[k]
        block_arrived(j, off(b, 2 * d - 1), plane[k], br_sem.at[j, d, k])
        send_block(j, off(b, 2 * d - 1), plane[k], bs_sem.at[j, 2, k], br_sem.at[j, 2, k], b_dev[1 + 2 * d])

    def b_three(j):
        for k in range(4):
            d = 1 - SIDES[k]
            block_arrived(j, off(b, 2 * d - 1), plane[k], br_sem.at[j, d, k])
            block_arrived(j, off(b, 2), plane[k], br_sem.at[j, 2, k])

    tokens = 64 * count

    def product(j, s):
        got = jnp.dot(cbuf[s], abuf[j][...].reshape(tokens, PARTS[j]), preferred_element_type=jnp.float32)
        got = (got * factor).astype(jnp.bfloat16)
        if s == 0:
            grecv[j][a] = got
        else:
            gsend[j][s] = got
            send(gsend[j].at[s], grecv[j].at[a], gs_sem.at[j, s], gr_sem.at[j, s], a_dev[4 - s])

    def inner(j):
        for s in (1, 2, 3):
            arrived(grecv[j].at[off(a, s)], gr_sem.at[j, s])

        def one(i, carry):
            span = pl.ds(pl.multiple_of(i * TILE, TILE), TILE)
            for q in range(4):
                where = pl.ds(q * quarter + STARTS[j], PARTS[j])
                gradient = grecv[j][q, span].astype(jnp.float32)
                new_first = (
                    beta_first * fbuf[span, where].astype(jnp.float32) + (1.0 - beta_first) * gradient
                ).astype(jnp.bfloat16)
                new_second = (
                    beta_second * sbuf[span, where].astype(jnp.float32)
                    + (1.0 - beta_second) * gradient * gradient
                ).astype(jnp.bfloat16)
                out_first[span, where] = new_first
                out_second[span, where] = new_second
                ratio = new_first.astype(jnp.float32) / (jnp.sqrt(new_second.astype(jnp.float32)) + epsilon)
                usend[j][q, span] = ratio.astype(jnp.bfloat16)
            urecv[j][rep, span] = usend[j][rep, span]
            return carry

        lax.fori_loop(0, rows // TILE, one, 0)
        for d in (2, 3, 1):
            send(usend[j].at[off(rep, d)], urecv[j].at[rep], us_sem.at[j, d - 1], ur_sem.at[j, d - 1], r_dev[d])

    def limits():
        for d in (1, 2, 3):
            arrived(ebuf.at[off(rep, -d)], er_sem.at[d - 1])
        loads[5].wait()
        blocks = ebuf.shape[1]
        span_of = lax.broadcasted_iota(jnp.int32, (blocks, quarter), 1) // (quarter // blocks)
        spread = (span_of == lax.broadcasted_iota(jnp.int32, (blocks, quarter), 0)).astype(jnp.float32).astype(jnp.bfloat16)
        for r in range(4):
            level = (clip_limit * jnp.exp2(ebuf[r].astype(jnp.float32))).astype(jnp.bfloat16)
            limbuf[r] = lax.dot_general(
                level, spread, (((0,), (0,)), ((), ())), preferred_element_type=jnp.float32
            ).astype(jnp.bfloat16)

    def outer(j):
        for d in (1, 2, 3):
            arrived(urecv[j].at[off(rep, -d)], ur_sem.at[j, d - 1])

        def one(i, carry):
            span = pl.ds(pl.multiple_of(i * TILE, TILE), TILE)
            where = pl.ds(STARTS[j], PARTS[j])
            weight = wbuf[span, where].astype(jnp.float32)
            total = jnp.zeros_like(weight)
            for r in range(4):
                delta = inner_rate * (urecv[j][r, span].astype(jnp.float32) + decay_rate * weight)
                limit = limbuf[r, span, where].astype(jnp.float32)
                total = total + jnp.minimum(jnp.maximum(delta, -limit), limit)
            pseudo = total * 0.25
            new_mom = outer_beta * mbuf[span, where] + pseudo
            out_mom[span, where] = new_mom
            out_weight[span, where] = (weight - outer_rate * (pseudo + outer_beta * new_mom)).astype(jnp.bfloat16)
            return carry

        lax.fori_loop(0, rows // TILE, one, 0)

    def moments():
        for copy in loads[1:5]:
            copy.wait()

    act_out(0)
    act_out(1)
    act_out(2)
    act_out(3)
    cot_out(0)
    z_one(1)
    cot_out(1)
    z_one(3)
    z_one(2)
    cot_one(0)
    b_one(3, 0)
    z_two(3)
    b_one(3, 1)
    cot_one(1)
    b_one(3, 2)
    z_two(2)
    z_one(0)
    b_one(2, 2)
    b_one(2, 1)
    limits()
    b_one(2, 0)
    z_three(3)
    cot_two()
    b_two(3, 2)
    b_one(3, 3)
    z_two(1)
    b_two(2, 1)
    z_three(2)
    b_one(1, 1)
    b_two(3, 0)
    b_one(2, 3)
    b_two(3, 1)
    b_two(2, 2)
    b_two(3, 3)
    b_one(1, 2)
    z_two(0)
    b_two(2, 0)
    b_one(0, 2)
    b_one(1, 0)
    b_three(3)
    b_one(0, 1)
    loads[0].wait()
    product(3, 1)
    z_three(1)
    cot_three()
    b_two(1, 1)
    b_one(1, 3)
    b_two(2, 3)
    product(3, 0)
    product(3, 3)
    b_two(1, 2)
    z_three(0)
    b_two(1, 0)
    product(3, 2)
    b_one(0, 3)
    b_two(1, 3)
    b_one(0, 0)
    b_three(2)
    product(2, 3)
    product(2, 0)
    product(2, 1)
    b_two(0, 2)
    product(2, 2)
    moments()
    inner(3)
    b_two(0, 1)
    b_three(1)
    b_two(0, 3)
    product(1, 3)
    product(1, 0)
    b_two(0, 0)
    product(1, 2)
    product(1, 1)
    inner(2)
    b_three(0)
    product(0, 3)
    product(0, 1)
    product(0, 2)
    inner(1)
    product(0, 0)
    outer(3)
    outer(2)
    inner(0)
    outer(1)
    outer(0)
    for copy in pending:
        copy.wait_send()


def flush(*refs):
    count = (len(refs) - 1) // 2
    sem = refs[-1]
    copies = [pltpu.make_async_copy(refs[i], refs[count + i], sem.at[i]) for i in range(count)]
    for copy in copies:
        copy.start()
    for copy in copies:
        copy.wait()


def expo_own(expo, q):
    blocks = expo.shape[0] // 4
    return expo.at[pl.ds(pl.multiple_of(q * blocks, blocks), blocks)]


def shards(activations, cotangent, weight, first_moment, second_moment, momentum, exponents):
    act, cot, first, second = activations[0], cotangent[0], first_moment[0], second_moment[0]
    expo = exponents[0].T
    rows, width = first.shape
    count, tokens = act.shape[0], cot.shape[1]
    quarter = weight.shape[1]
    bf16, f32 = jnp.bfloat16, jnp.float32
    dma = pltpu.SemaphoreType.DMA
    results = (
        (weight.shape, bf16),
        (momentum.shape, f32),
        (first.shape, bf16),
        (second.shape, bf16),
    )
    pieces = [pltpu.VMEM((4, rows, part), bf16) for part in PARTS]
    held = pl.pallas_call(
        kernel,
        out_shape=tuple(pltpu.VMEM(*r) for r in results),
        in_specs=[pl.BlockSpec(memory_space=pltpu.HBM)] * 7,
        out_specs=(pl.BlockSpec(memory_space=pltpu.VMEM),) * 4,
        scratch_shapes=[
            pltpu.VMEM((4, rows, tokens), bf16),
            [pltpu.VMEM((4, 4, 4, count, part), bf16) for part in PARTS],
            pltpu.VMEM((rows, width), bf16),
            pltpu.VMEM((rows, width), bf16),
            pltpu.VMEM((rows, quarter), bf16),
            pltpu.VMEM((rows, quarter), f32),
            pieces, pieces, pieces, pieces,
            pltpu.VMEM((4, expo.shape[0] // 4, rows), jnp.int32),
            pltpu.VMEM((4, rows, quarter), bf16),
            dma((6,)), dma((CHUNKS,)),
            dma((6,)), dma((6,)),
            dma((CHUNKS, 3)), dma((CHUNKS, 3)),
            dma((CHUNKS, 3)), dma((CHUNKS, 3)),
            dma((CHUNKS, 3, 4)), dma((CHUNKS, 3, 4)),
            dma((CHUNKS, 4)), dma((CHUNKS, 4)),
            dma((CHUNKS, 3)), dma((CHUNKS, 3)),
            dma((3,)), dma((3,)),
        ],
        compiler_params=pltpu.CompilerParams(
            collective_id=0, has_side_effects=True, vmem_limit_bytes=40 * 1024 * 1024
        ),
        cost_estimate=pl.CostEstimate(
            flops=2 * rows * tokens * width, bytes_accessed=14_000_000, transcendentals=rows * width
        ),
    )(*(pltpu.with_memory_space_constraint(v, pltpu.HBM) for v in (act, cot, weight, first, second, momentum, expo)))
    new_weight, new_mom, new_first, new_second = pl.pallas_call(
        flush,
        out_shape=tuple(jax.ShapeDtypeStruct(*r) for r in results),
        in_specs=[pl.BlockSpec(memory_space=pltpu.VMEM)] * 4,
        out_specs=(pl.BlockSpec(memory_space=pltpu.HBM),) * 4,
        scratch_shapes=[dma((4,))],
        compiler_params=pltpu.CompilerParams(vmem_limit_bytes=2 * 1024 * 1024),
    )(*(pltpu.with_memory_space_constraint(v, pltpu.VMEM) for v in held))
    return (new_weight, new_mom, new_first[None], new_second[None])


def solution(mesh):
    in_specs = (
        P("rep", "fsdp", None),
        P("rep", "fsdp", None),
        P("fsdp", "rep"),
        P("rep", "fsdp", None),
        P("rep", "fsdp", None),
        P("fsdp", "rep"),
        P("rep", "fsdp", None),
    )
    out_specs = (P("fsdp", "rep"), P("fsdp", "rep"), P("rep", "fsdp", None), P("rep", "fsdp", None))
    return jax.shard_map(shards, mesh=mesh, in_specs=in_specs, out_specs=out_specs, check_vma=False)
```

time: 102 us -> 89.1 us (0.87)
  local copies, waits for them, and re-layouts: 9.13 us -> 0 us
  Pallas kernels: 92.3 us -> 88.4 us
    unnamed x14 -> x0, local copies, waits for them, and re-layouts: 9.13 us -> none
    pallas_call x1 -> x2, Pallas kernels: 92.3 us -> 88.4 us  [the longest x1 86 us: shards(): pl.pallas_call(kernel, out_shape=tuple((pltpu.VMEM(*r) for r in results))...]
where the time goes in v2:
time: 89.1 us; the launch traced here: 89 us
  Pallas kernels  88.4 us (99%)
    pallas_call x1, Pallas kernels, shards(): pl.pallas_call(kernel, out_shape=tuple((pltpu.VMEM(*r) for r in results))...  86 us
    pallas_call x1, Pallas kernels, shards(): pl.pallas_call(flush, out_shape=tuple((jax.ShapeDtypeStruct(*r) for r in...  2.32 us

profile of v2, /device:TPU:1, one launch (start us, length us, event | category | flops | bytes accessed | tf_op | source)
XLA Modules:
  0.0 89.0 jit_solution(975383188989217633)
XLA Ops:
  0.6 86.0 %shard_map.102 = (bf16[224,1024]{1,0:T(8,128)(2,1)S(1)}, f32[224,1024]{1,0:T(8,128)S(1)}, bf16[224,4096]{1,0:T(8,128)(2,1)S(1)}, bf16[224,4096]{1,0:T(8,128)(2,1)S(1)}) custom-call(bf16[48,4096]{1,0:T(8,128)(2,1)} %bitcast.14, bf16[224,3072]{1,0:T(8,128)(2,1)} %bitcast.13, bf16[224,1024]{1,0:T(8,128)(2,1)} %wgt.1, bf16[224,4096]{1,0:T(8,128)(2,1)} %bitcast.9, ...), custom_call_target="tpu_custom_call" | custom-call | flops 5637144576 | bytes 14000000 | tf_op jit(solution)/shard_map/pallas_call | solution.py:377
  86.7 2.3 %shard_map.103 = (bf16[224,1024]{1,0:T(8,128)(2,1)}, f32[224,1024]{1,0:T(8,128)}, bf16[224,4096]{1,0:T(8,128)(2,1)}, bf16[224,4096]{1,0:T(8,128)(2,1)}) custom-call(bf16[224,1024]{1,0:T(8,128)(2,1)S(1)} %get-tuple-element.12.refs_0_, f32[224,1024]{1,0:T(8,128)S(1)} %get-tuple-element.13.refs_1_, bf16[224,4096]{1,0:T(8,128)(2,1)S(1)} %get-tuple-element.14.refs_2_, ...), custom_call_target="tpu_custom_call" | custom-call | tf_op jit(solution)/shard_map/pallas_call | solution.py:408

commit v3 on v2

--- a/solution.py
+++ b/solution.py
@@ -71,7 +71,7 @@
     ]
 
     def unit(j, a_, b_, z_):
-        return abuf[j].at[b_ * (1 - c) + a_ * c, z_, a_ * (1 - c) + b_ * c]
+        return abuf[j].at[b_, z_, a_]
 
     own = [
         pltpu.make_async_copy(
@@ -116,22 +116,11 @@
     for d in (1, 2, 3):
         send(expo_own(expo, off(rep, d)), ebuf.at[rep], es_sem.at[d - 1], er_sem.at[d - 1], r_dev[d])
 
-    def block(j, b_, z_, role):
-        return abuf[j].at[b_, z_] if role == 0 else abuf[j].at[:, z_, b_]
-
     def send_block(j, b_, z_, ssem, rsem, dev):
-        for role in (0, 1):
-            @pl.when(c == role)
-            def _(role=role):
-                ref = block(j, b_, z_, role)
-                remote(ref, ref, ssem, rsem, dev).start()
-        pending.append(remote(block(j, b_, z_, 0), block(j, b_, z_, 0), ssem, rsem, dev))
+        send(abuf[j].at[b_, z_], abuf[j].at[b_, z_], ssem, rsem, dev)
 
     def block_arrived(j, b_, z_, rsem):
-        for role in (0, 1):
-            @pl.when(c == role)
-            def _(role=role):
-                arrived(block(j, b_, z_, role), rsem)
+        arrived(abuf[j].at[b_, z_], rsem)
 
     def z_one(j):
         own[j].wait()
@@ -179,10 +168,15 @@
             block_arrived(j, off(b, 2 * d - 1), plane[k], br_sem.at[j, d, k])
             block_arrived(j, off(b, 2), plane[k], br_sem.at[j, 2, k])
 
-    tokens = 64 * count
+    group = 16 * count
 
     def product(j, s):
-        got = jnp.dot(cbuf[s], abuf[j][...].reshape(tokens, PARTS[j]), preferred_element_type=jnp.float32)
+        def one(p, total):
+            held = [abuf[j][p * (1 - c) + q * c, k, q * (1 - c) + p * c] for k in range(4) for q in range(4)]
+            mine = cbuf[s, :, pl.ds(pl.multiple_of(p * group, 128), group)]
+            return total + jnp.dot(mine, jnp.concatenate(held, axis=0), preferred_element_type=jnp.float32)
+
+        got = lax.fori_loop(0, 4, one, jnp.zeros((rows, PARTS[j]), jnp.float32))
         got = (got * factor).astype(jnp.bfloat16)
         if s == 0:
             grecv[j][a] = got
@@ -335,9 +329,9 @@
     product(0, 2)
     inner(1)
     product(0, 0)
+    inner(0)
     outer(3)
     outer(2)
-    inner(0)
     outer(1)
     outer(0)
     for copy in pending:

time: 89.1 us -> 89.5 us (level)
  no operation moved by 1% of the time
where the time goes in v3:
time: 89.5 us; the launch traced here: 89.4 us
  Pallas kernels  88.8 us (99%)
    pallas_call x1, Pallas kernels, shards(): pl.pallas_call(kernel, out_shape=tuple((pltpu.VMEM(*r) for r in results))...  86.4 us
    pallas_call x1, Pallas kernels, shards(): pl.pallas_call(flush, out_shape=tuple((jax.ShapeDtypeStruct(*r) for r in...  2.32 us

profile of v3, /device:TPU:1, one launch (start us, length us, event | category | flops | bytes accessed | tf_op | source)
XLA Modules:
  0.0 89.4 jit_solution(17829847742278169567)
XLA Ops:
  0.6 86.4 %shard_map.102 = (bf16[224,1024]{1,0:T(8,128)(2,1)S(1)}, f32[224,1024]{1,0:T(8,128)S(1)}, bf16[224,4096]{1,0:T(8,128)(2,1)S(1)}, bf16[224,4096]{1,0:T(8,128)(2,1)S(1)}) custom-call(bf16[48,4096]{1,0:T(8,128)(2,1)} %bitcast.14, bf16[224,3072]{1,0:T(8,128)(2,1)} %bitcast.13, bf16[224,1024]{1,0:T(8,128)(2,1)} %wgt.1, bf16[224,4096]{1,0:T(8,128)(2,1)} %bitcast.9, ...), custom_call_target="tpu_custom_call" | custom-call | flops 5637144576 | bytes 14000000 | tf_op jit(solution)/shard_map/pallas_call | solution.py:371
  87.1 2.3 %shard_map.103 = (bf16[224,1024]{1,0:T(8,128)(2,1)}, f32[224,1024]{1,0:T(8,128)}, bf16[224,4096]{1,0:T(8,128)(2,1)}, bf16[224,4096]{1,0:T(8,128)(2,1)}) custom-call(bf16[224,1024]{1,0:T(8,128)(2,1)S(1)} %get-tuple-element.12.refs_0_, f32[224,1024]{1,0:T(8,128)S(1)} %get-tuple-element.13.refs_1_, bf16[224,4096]{1,0:T(8,128)(2,1)S(1)} %get-tuple-element.14.refs_2_, ...), custom_call_target="tpu_custom_call" | custom-call | tf_op jit(solution)/shard_map/pallas_call | solution.py:402
